TPU v7x, 256 devices: a whole 4x4x8 slice. The times are simulated.
256 devices in a mesh: dp: 16 (over y_hi, x, core), mp: 16 (over y_lo, z).
Axes of the slice: x: 4, y: 4 (y_hi: 2, y_lo: 2; y = y_hi * 2 + y_lo), z: 8, core: 2. Of those that a mesh axis runs over, the one named last changes fastest.
Arguments:
- activations: bfloat16 [4096, 4096], P('dp', 'mp'), may hold values from -6 to 6
- output_grads: bfloat16 [4096, 32768], P('dp', 'mp'), may hold values from -0.09375 to 0.09375
- owners: int32 [16, 16], replicated, may hold values from 0 to 15, as said below
- statistics: float32 [16, 16, 1024, 1024], P('mp', 'dp'), may hold values from -3 to 8
- inv_roots: bfloat16 [16, 16, 1024, 1024], P('mp', 'dp'), may hold values from -3 to 6
Outputs:
- new_statistics: float32 [16, 16, 1024, 1024], P('mp', 'dp')
- preconditioned: bfloat16 [4096, 32768], P('dp', 'mp')
Inputs may be any that keep to these rules, and one draw needn't show every extreme that they name: `owners`: each row holds every number of 0 to 15 once; entries 2b and 2b + 1 are 2k and 2k + 1 in some order, for some k.
All inputs are finite; a program needn't handle non-finite values.
Results may differ from a plain program's by a relative error of at most 0.024.
Values may be sent and summed in bfloat16 or wider, within the bound.
No kernel may reach another device: no remote copies, remote signals or barrier semaphores. Data moves between devices by JAX's collectives and lax.ppermute only.
A program may use at most 128 MiB of HBM per device.

v0:
```python
import jax
import jax.numpy as jnp
from jax import lax
from jax.sharding import PartitionSpec as P

D = 4096
BLK = 1024
decay_rate = 0.9


def from_partner(x, axis, distance):
    return lax.ppermute(x, axis, [(i, i ^ 1 << distance) for i in range(lax.axis_size(axis))])


def owner_layout(owner_table, devices):
    mp_index = lax.axis_index("mp")
    table_row = lax.dynamic_index_in_dim(owner_table, mp_index, 0, keepdims=False)
    slots = jnp.arange(devices, dtype=jnp.int32)
    match = (table_row[None, :] == slots[:, None]).astype(jnp.int32)
    position = jnp.sum(match * slots[None, :], axis=1)
    return (table_row, position)


def on_device(activations, output_grads, owners, statistics, inv_roots):
    devices = lax.axis_size("dp")
    col_blocks = output_grads.shape[1] // BLK
    half_rows = BLK // 2
    rows_dev = D // devices
    table_row, position = owner_layout(owners, devices)
    my_index = lax.axis_index("dp")
    my_position = position[my_index]
    left_side = my_position % 2 == 0
    my_block = my_position // 2
    parity = my_index % 2
    all_features = lax.all_gather(activations, "mp", axis=1, tiled=True)
    owner_ids = jnp.arange(devices, dtype=jnp.int32)
    owner_block = position // 2
    owner_rows = owner_block // col_blocks * BLK + owner_ids % 2 * half_rows
    owner_cols = owner_block % col_blocks * BLK

    def select_parts(owner_index):
        feature_part = lax.dynamic_slice_in_dim(all_features, owner_rows[owner_index], half_rows, 1)
        grad_part = lax.dynamic_slice_in_dim(output_grads, owner_cols[owner_index], BLK, 1)
        return (feature_part, grad_part)

    def owner_term(owner_index):
        feature_part, grad_part = select_parts(owner_index)
        return lax.dot_general(
            feature_part, grad_part, (((0,), (0,)), ((), ())), preferred_element_type=jnp.float32
        )

    picked = jnp.arange(half_rows * lax.axis_size("dp") // half_rows, dtype=jnp.int32)
    summed = lax.psum_scatter(
        jax.vmap(owner_term)(picked)
        .reshape(half_rows * lax.axis_size("dp"), BLK)
        .astype(jnp.bfloat16),
        "dp",
        scatter_dimension=0,
        tiled=True,
    )
    other_half = from_partner(summed, "dp", 0)
    block_grad = jnp.where(
        parity == 0,
        jnp.concatenate([summed, other_half], 0),
        jnp.concatenate([other_half, summed], 0),
    )
    old_stat = statistics[0, 0]
    gram_matrix = lax.cond(
        left_side,
        lambda: lax.dot_general(
            block_grad, block_grad, (((1,), (1,)), ((), ())), preferred_element_type=jnp.float32
        ),
        lambda: lax.dot_general(
            block_grad, block_grad, (((0,), (0,)), ((), ())), preferred_element_type=jnp.float32
        ),
    )
    new_stat = decay_rate * old_stat + (1.0 - decay_rate) / BLK * gram_matrix
    own_root = inv_roots[0, 0]
    payload = lax.cond(
        left_side,
        lambda: jnp.dot(own_root, block_grad, preferred_element_type=jnp.float32).astype(
            jnp.bfloat16
        ),
        lambda: own_root,
    )
    received = from_partner(payload, "dp", 0)
    left_product = jnp.where(left_side, payload, received)
    right_root = jnp.where(left_side, received, own_root)
    columns = lax.dynamic_slice_in_dim(right_root, parity * half_rows, half_rows, 1)
    result_part = jnp.dot(left_product, columns, preferred_element_type=jnp.float32).astype(
        jnp.bfloat16
    )
    block_row = my_block // col_blocks
    row_block = my_index * rows_dev // BLK
    pair_bases = 2 * (table_row[0::2] // 2)
    wanted = row_block * col_blocks + jnp.arange(col_blocks, dtype=jnp.int32)
    sources = (
        jnp.take(pair_bases, wanted)[:, None] + jnp.arange(2, dtype=jnp.int32)[None, :]
    ).reshape(-1)
    pieces = result_part.reshape(BLK // rows_dev, rows_dev, half_rows)
    outgoing = jnp.zeros((devices, rows_dev, half_rows), jnp.bfloat16)
    outgoing = lax.dynamic_update_slice_in_dim(outgoing, pieces, block_row * (BLK // rows_dev), 0)
    incoming = lax.all_to_all(outgoing, "dp", split_axis=0, concat_axis=2, tiled=True)
    incoming = incoming.reshape(rows_dev, devices, half_rows)
    gathered = jnp.take(incoming, sources, axis=1)
    preconditioned = gathered.reshape(rows_dev, col_blocks * BLK)
    return (new_stat[None, None], preconditioned)


def solution(mesh):
    in_specs = (
        P("dp", "mp"),
        P("dp", "mp"),
        P(),
        P("mp", "dp", None, None),
        P("mp", "dp", None, None),
    )
    out_specs = (P("mp", "dp", None, None), P("dp", "mp"))
    return jax.shard_map(
        on_device, mesh=mesh, in_specs=in_specs, out_specs=out_specs, check_vma=False
    )
```

profile of v0, /device:TPU:2, one launch (start us, length us, event | category | flops | bytes accessed | tf_op | source)
XLA Modules:
  0.0 399.0 jit_solution(15943701818986518734)
XLA Ops:
  9.5 53.0 %while.3 = (s32[]{:T(128)}, bf16[256,2048]{1,0:T(8,128)(2,1)}, s32[16,2]{0,1:T(2,128)S(1)}, bf16[16,256,1024]{2,1,0:T(8,128)(2,1)}, s32[]{:T(128)}) while((s32[]{:T(128)}, bf16[256,2048]{1,0:T(8,128)(2,1)}, s32[16,2]{0,1:T(2,128)S(1)}, bf16[16,256,1024]{2,1,0:T(8,128)(2,1)}, s32[]{:T(128)}) %tuple.48), condition=%wide.while_cond.1, body=%wide.while_body.1.sunk | while | flops 2 | bytes 1049689 | solution.py:43
  16.8 2.7 bitcast_dynamic-update-slice_fusion.5
  23.4 2.7 bitcast_dynamic-update-slice_fusion.5
  26.7 2.7 bitcast_dynamic-update-slice_fusion.5
  36.7 2.7 bitcast_dynamic-update-slice_fusion.5
  40.0 2.7 bitcast_dynamic-update-slice_fusion.5
  43.3 2.7 bitcast_dynamic-update-slice_fusion.5
  46.7 2.7 bitcast_dynamic-update-slice_fusion.5
  59.9 2.7 bitcast_dynamic-update-slice_fusion.5
  62.6 22.1 %all-gather.2.cloned.1.call-done = bf16[256,4096]{1,0:T(8,128)(2,1)} async-done(((bf16[256,256]{1,0:T(8,128)(2,1)}), bf16[256,4096]{1,0:T(8,128)(2,1)}) %all-gather.2.cloned.1.call-update) | async-done | bytes 2097168 | tf_op jit(solution)/shard_map/all_gather | solution.py:35
  87.1 48.7 %while.2 = (s32[]{:T(128)}, bf16[256,4096]{1,0:T(8,128)(2,1)}, s32[16,2]{0,1:T(2,128)S(1)}, bf16[16,256,512]{2,1,0:T(8,128)(2,1)}, s32[]{:T(128)}) while((s32[]{:T(128)}, bf16[256,4096]{1,0:T(8,128)(2,1)}, s32[16,2]{0,1:T(2,128)S(1)}, bf16[16,256,512]{2,1,0:T(8,128)(2,1)}, s32[]{:T(128)}) %tuple.45), condition=%wide.while_cond, body=%wide.while_body.sunk | while | flops 2 | bytes 525401 | solution.py:42
  135.8 12.2 %convolution_convert_fusion.1 = bf16[16,512,1024]{2,1,0:T(8,128)(2,1)} fusion(bf16[16,256,512]{2,1,0:T(8,128)(2,1)} %get-tuple-element.24, bf16[16,256,1024]{2,1,0:T(8,128)(2,1)} %get-tuple-element.32), kind=kOutput, calls=%fused_computation.9 | convolution fusion | flops 4303355904 | bytes 29360128 | tf_op jit(solution)/shard_map/vmap()/dot_general | solution.py:48
  148.0 153.9 %reduce-scatter.2.cloned.1.call-done = bf16[512,1024]{1,0:T(8,128)(2,1)} async-done(((bf16[8192,1024]{1,0:T(8,128)(2,1)}), bf16[512,1024]{1,0:T(8,128)(2,1)}) %reduce-scatter.2.cloned.1.call-update) | async-done | bytes 1048592 | tf_op jit(solution)/shard_map/reduce_scatter | solution.py:53
  304.7 3.9 maximum_select_fusion
  308.6 5.3 %conditional.3 = (bf16[1024,1024]{1,0:T(8,128)(2,1)}) conditional(s32[]{:T(128)} %convert_element_type.17, bf16[1024,1024]{1,0:T(8,128)(2,1)S(1)} %bitcast.56, (bf16[1024,1024]{1,0:T(8,128)(2,1)S(1)}, bf16[1024,1024]{1,0:T(8,128)(2,1)}) %tuple.59), branch_computations={%region_4.5_spmd, %region_5.6_spmd} | conditional | flops 2148532224 | bytes 6291464 | solution.py:79
  308.6 5.3 %convolution_convert_fusion = bf16[1024,1024]{1,0:T(8,128)(2,1)} fusion(bf16[1024,1024]{1,0:T(8,128)(2,1)S(1)} %get-tuple-element.13, bf16[1024,1024]{1,0:T(8,128)(2,1)} %get-tuple-element.14), kind=kOutput, calls=%fused_computation.4 | convolution fusion | flops 2148532224 | bytes 6291456 | tf_op jit(solution)/shard_map/cond/branch_1_fun/dot_general | solution.py:81
  314.6 3.8 collective-permute-done.1
  318.4 3.2 fusion.4
  325.1 6.2 %all-to-all-start = ((bf16[16,256,512]{2,1,0:T(8,128)(2,1)}), bf16[16,256,512]{2,1,0:T(8,128)(2,1)}, u32[]{:S(2)}, u32[]{:S(2)}) async-start(bf16[16,256,512]{2,1,0:T(8,128)(2,1)} %constant_dynamic-update-slice_fusion), calls=%async_computation.1 | async-start | bytes 8388608 | tf_op jit(solution)/shard_map/all_to_all | solution.py:103
  332.3 4.6 %conditional.2 = (f32[1024,1024]{1,0:T(8,128)}) conditional(s32[]{:T(128)} %convert_element_type.17, bf16[1024,1024]{1,0:T(8,128)(2,1)S(1)} %copy-done.3, bf16[1024,1024]{1,0:T(8,128)(2,1)S(1)} %copy-done.3), branch_computations={%region_2.3_spmd, %region_3.4_spmd} | conditional | flops 2147483648 | bytes 6291464 | solution.py:68
  332.5 4.4 %fusion.18 = f32[1024,1024]{1,0:T(8,128)} fusion(bf16[1024,1024]{1,0:T(8,128)(2,1)S(1)} %param.1), kind=kOutput, calls=%fused_computation.61 | convolution fusion | flops 2147483648 | bytes 6291456 | tf_op jit(solution)/shard_map/cond/branch_1_fun/dot_general | solution.py:70
  336.9 7.0 %fusion = f32[1,1,1024,1024]{3,2,1,0:T(8,128)} fusion(f32[1024,1024]{1,0:T(8,128)} %get-tuple-element.131, f32[1,1,1024,1024]{3,2,1,0:T(8,128)} %param.12), kind=kLoop, calls=%fused_computation.11 | loop fusion | flops 3145728 | bytes 12582912 | tf_op jit(solution)/shard_map/broadcast_in_dim | solution.py:107
  343.9 44.2 %all-to-all-done = bf16[16,256,512]{2,1,0:T(8,128)(2,1)} async-done(((bf16[16,256,512]{2,1,0:T(8,128)(2,1)}), bf16[16,256,512]{2,1,0:T(8,128)(2,1)}, u32[]{:S(2)}, u32[]{:S(2)}) %all-to-all-start) | async-done | bytes 4194336 | tf_op jit(solution)/shard_map/all_to_all | solution.py:103
  388.1 2.8 gather_fusion.3
  (136 shorter events, 91.3 us)
Async XLA Ops:
  7.2 0.8 copy-start
  7.2 77.5 %all-gather.2.cloned.1.call-start = ((), (), s32[]{:S(2)}) async-start(), calls=%async_computation.2 | async-start | bytes 2228224 | tf_op jit(solution)/shard_map/all_gather | solution.py:35
  7.9 294.0 %reduce-scatter.2.cloned.1.call-start = ((), (), s32[]{:S(2)}) async-start(), calls=%async_computation.3 | async-start | bytes 17825792 | tf_op jit(solution)/shard_map/reduce_scatter | solution.py:53
  148.0 160.6 %copy-start.2 = (bf16[1,1,1024,1024]{3,2,1,0:T(8,128)(2,1)S(1)}, bf16[1,1,1024,1024]{3,2,1,0:T(8,128)(2,1)}, u32[]{:S(2)}) copy-start(bf16[1,1,1024,1024]{3,2,1,0:T(8,128)(2,1)} %param.13) | copy-start | bytes 6291460
  301.9 2.9 collective-permute-start
  313.9 4.5 %collective-permute-start.1 = (bf16[1024,1024]{1,0:T(8,128)(2,1)}, bf16[1024,1024]{1,0:T(8,128)(2,1)}, u32[]{:S(2)}, u32[]{:S(2)}) collective-permute-start(bf16[1024,1024]{1,0:T(8,128)(2,1)} %get-tuple-element.132), channel_id=1, source_target_pairs={{0,16},{16,0},{32,48},{48,32},{64,80},{80,64},{96,112},{112,96},{1... | collective-permute-start | bytes 6291464 | tf_op jit(solution)/shard_map/ppermute | solution.py:12
  325.1 7.3 %copy-start.3 = (bf16[1024,1024]{1,0:T(8,128)(2,1)S(1)}, bf16[1024,1024]{1,0:T(8,128)(2,1)}, u32[]{:S(2)}) copy-start(bf16[1024,1024]{1,0:T(8,128)(2,1)} %maximum_select_fusion) | copy-start | bytes 6291460
  325.1 63.1 %all-to-all-start = ((bf16[16,256,512]{2,1,0:T(8,128)(2,1)}), bf16[16,256,512]{2,1,0:T(8,128)(2,1)}, u32[]{:S(2)}, u32[]{:S(2)}) async-start(bf16[16,256,512]{2,1,0:T(8,128)(2,1)} %constant_dynamic-update-slice_fusion), calls=%async_computation.1 | async-start | bytes 8388608 | tf_op jit(solution)/shard_map/all_to_all | solution.py:103
  336.9 55.2 %copy-start.1 = (s32[16,16]{1,0:T(8,128)S(1)}, s32[16,16]{1,0:T(8,128)}, u32[]{:S(2)}) copy-start(s32[16,16]{1,0:T(8,128)} %param.11) | copy-start | bytes 3076
Sparse Core Ops, SparseCore 0:
  9.7 74.9 all-gather.1
  148.1 153.6 reduce-scatter.1
where the time goes:
time: 401 us; the launch traced here: 399 us
  waiting for transfers between devices  225 us (56%)
  local copies, waits for them, and re-layouts  113 us (28%)
  matrix products  25 us (6%)
  between operations  16.9 us (4%)
  other arithmetic  12.2 us (3%)
  starting transfers between devices  6.23 us (2%)
    reduce_scatter x1, waiting for transfers between devices, on_device(): lax.psum_scatter(jax.vmap(owner_term)(picked).reshape(half_rows * lax.axi...  154 us
    gather x96, local copies, waits for them, and re-layouts  102 us
    all_to_all x1, waiting for transfers between devices, on_device(): lax.all_to_all(outgoing, 'dp', split_axis=0, concat_axis=2, tiled=True)  44.2 us
    all_gather x1, waiting for transfers between devices, on_device(): all_features = lax.all_gather(activations, 'mp', axis=1, tiled=True)  22.1 us
    dot_general x1, matrix products, owner_term(): lax.dot_general(feature_part, grad_part, (((0,), (0,)), ((), ())), prefer...  12.2 us
  transfers between devices with their start and end apart: 5, of which 5 were waited for; matrix products, arithmetic and copies ran while one was open for 17% of the time, Pallas kernels for 0%

commit v1 on v0

--- a/solution.py
+++ b/solution.py
@@ -32,7 +32,10 @@
     left_side = my_position % 2 == 0
     my_block = my_position // 2
     parity = my_index % 2
-    all_features = lax.all_gather(activations, "mp", axis=1, tiled=True)
+    all_features = jnp.concatenate(
+        lax.all_to_all(jnp.stack([activations for _ in range(lax.axis_size("mp"))]), "mp", 0, 0),
+        axis=1,
+    )
     owner_ids = jnp.arange(devices, dtype=jnp.int32)
     owner_block = position // 2
     owner_rows = owner_block // col_blocks * BLK + owner_ids % 2 * half_rows

time: 401 us -> 386 us (0.963)
  waiting for transfers between devices: 225 us -> 212 us
  local copies, waits for them, and re-layouts: 113 us -> 103 us
  starting transfers between devices: 6.23 us -> 15.8 us
    all_gather x1 -> x0, waiting for transfers between devices: 22.1 us -> none  [on_device(): all_features = lax.all_gather(activations, 'mp', axis=1, tiled=True)]
    gather x96 -> x128, local copies, waits for them, and re-layouts: 102 us -> 86.2 us
    all_to_all x0 -> x1, waiting for transfers between devices: none -> 10.8 us  [on_device(): lax.all_to_all(jnp.stack([activations for _ in range(lax.axis_size('mp'))...]
    all_to_all x0 -> x1, starting transfers between devices: none -> 9.58 us  [on_device(): lax.all_to_all(jnp.stack([activations for _ in range(lax.axis_size('mp'))...]
  transfers between devices with their start and end apart: 5 -> 5, of which waited for: 5 -> 5; matrix products, arithmetic and copies ran while one was open for 17% -> 13% of each run, Pallas kernels for 0% -> 0%
where the time goes in v1:
time: 386 us; the launch traced here: 385 us
  waiting for transfers between devices  212 us (55%)
  local copies, waits for them, and re-layouts  103 us (27%)
  matrix products  25 us (6%)
  between operations  16.9 us (4%)
  starting transfers between devices  15.8 us (4%)
  other arithmetic  12.2 us (3%)
    reduce_scatter x1, waiting for transfers between devices, on_device(): lax.psum_scatter(jax.vmap(owner_term)(picked).reshape(half_rows * lax.axi...  153 us
    gather x128, local copies, waits for them, and re-layouts  86.2 us
    all_to_all x1, waiting for transfers between devices, on_device(): lax.all_to_all(outgoing, 'dp', split_axis=0, concat_axis=2, tiled=True)  44.2 us
    dot_general x1, matrix products, owner_term(): lax.dot_general(feature_part, grad_part, (((0,), (0,)), ((), ())), prefer...  12.2 us
    all_to_all x1, waiting for transfers between devices, on_device(): lax.all_to_all(jnp.stack([activations for _ in range(lax.axis_size('mp'))...  10.8 us
    all_to_all x1, starting transfers between devices, on_device(): lax.all_to_all(jnp.stack([activations for _ in range(lax.axis_size('mp'))...  9.58 us
  transfers between devices with their start and end apart: 5, of which 5 were waited for; matrix products, arithmetic and copies ran while one was open for 13% of the time, Pallas kernels for 0%

profile of v1, /device:TPU:2, one launch (start us, length us, event | category | flops | bytes accessed | tf_op | source)
XLA Modules:
  0.0 385.1 jit_solution(13073659282532014347)
XLA Ops:
  7.2 2.5 stack.2
  9.7 9.6 %all-to-all-start = ((bf16[16,256,256]{2,1,0:T(8,128)(2,1)}), bf16[16,256,256]{2,1,0:T(8,128)(2,1)S(1)}, u32[]{:S(2)}, u32[]{:S(2)}) async-start(bf16[16,256,256]{2,1,0:T(8,128)(2,1)} %stack.2), calls=%async_computation | async-start | bytes 4194304 | tf_op jit(solution)/shard_map/all_to_all | solution.py:36
  20.9 36.6 %while.3 = (s32[]{:T(128)}, bf16[256,2048]{1,0:T(8,128)(2,1)S(1)}, s32[16,2]{0,1:T(2,128)S(1)}, bf16[16,256,1024]{2,1,0:T(8,128)(2,1)}, s32[]{:T(128)}) while((s32[]{:T(128)}, bf16[256,2048]{1,0:T(8,128)(2,1)S(1)}, s32[16,2]{0,1:T(2,128)S(1)}, bf16[16,256,1024]{2,1,0:T(8,128)(2,1)}, s32[]{:T(128)}) %tuple.59), condition=%wide.while_cond.1, body=%wide.while_body.1.sunk | while | flops 2 | bytes 1049689 | solution.py:46
  26.1 1.7 bitcast_dynamic-update-slice_fusion.5
  44.4 1.7 bitcast_dynamic-update-slice_fusion.5
  55.8 1.7 bitcast_dynamic-update-slice_fusion.5
  57.5 10.8 %all-to-all-done = bf16[16,256,256]{2,1,0:T(8,128)(2,1)S(1)} async-done(((bf16[16,256,256]{2,1,0:T(8,128)(2,1)}), bf16[16,256,256]{2,1,0:T(8,128)(2,1)S(1)}, u32[]{:S(2)}, u32[]{:S(2)}) %all-to-all-start) | async-done | bytes 2097184 | tf_op jit(solution)/shard_map/all_to_all | solution.py:36
  68.3 2.4 copy.17
  70.7 2.4 broadcast.206.clone
  73.1 49.9 %while.2 = (s32[]{:T(128)}, bf16[256,4096]{0,1:T(8,128)(2,1)}, s32[16,2]{0,1:T(2,128)S(1)}, bf16[16,256,512]{2,1,0:T(8,128)(2,1)}, s32[]{:T(128)}) while((s32[]{:T(128)}, bf16[256,4096]{0,1:T(8,128)(2,1)}, s32[16,2]{0,1:T(2,128)S(1)}, bf16[16,256,512]{2,1,0:T(8,128)(2,1)}, s32[]{:T(128)}) %tuple.60), condition=%wide.while_cond, body=%wide.while_body.sunk | while | flops 2 | bytes 1573469 | solution.py:45
  123.0 12.2 %convolution_convert_fusion.1 = bf16[16,512,1024]{2,1,0:T(8,128)(2,1)} fusion(bf16[16,256,512]{2,1,0:T(8,128)(2,1)} %get-tuple-element.24, bf16[16,256,1024]{2,1,0:T(8,128)(2,1)} %get-tuple-element.32), kind=kOutput, calls=%fused_computation.10 | convolution fusion | flops 4303355904 | bytes 29360128 | tf_op jit(solution)/shard_map/vmap()/dot_general | solution.py:51
  135.2 152.8 %reduce-scatter.2.cloned.1.call-done = bf16[512,1024]{1,0:T(8,128)(2,1)} async-done(((bf16[8192,1024]{1,0:T(8,128)(2,1)}), bf16[512,1024]{1,0:T(8,128)(2,1)}) %reduce-scatter.2.cloned.1.call-update) | async-done | bytes 1048592 | tf_op jit(solution)/shard_map/reduce_scatter | solution.py:56
  290.8 3.9 %maximum_select_fusion = bf16[1024,1024]{1,0:T(8,128)(2,1)} fusion(bf16[512,1024]{1,0:T(8,128)(2,1)S(1)} %collective-permute-done, bf16[512,1024]{1,0:T(8,128)(2,1)} %reduce-scatter.2.cloned.1.call-done, pred[]{:T(512)S(6)} %eq.32), kind=kLoop, calls=%fused_computation.13 | loop fusion | flops 9437184 | bytes 4194305 | tf_op jit(solution)/shard_map/jit(_where)/select_n | solution.py:65
  294.8 5.3 %conditional.3 = (bf16[1024,1024]{1,0:T(8,128)(2,1)}) conditional(s32[]{:T(128)} %convert_element_type.17, bf16[1024,1024]{1,0:T(8,128)(2,1)S(1)} %bitcast.60, (bf16[1024,1024]{1,0:T(8,128)(2,1)S(1)}, bf16[1024,1024]{1,0:T(8,128)(2,1)}) %tuple.61), branch_computations={%region_4.5_spmd, %region_5.6_spmd} | conditional | flops 2148532224 | bytes 6291464 | solution.py:82
  294.8 5.3 %convolution_convert_fusion = bf16[1024,1024]{1,0:T(8,128)(2,1)} fusion(bf16[1024,1024]{1,0:T(8,128)(2,1)S(1)} %get-tuple-element.13, bf16[1024,1024]{1,0:T(8,128)(2,1)} %get-tuple-element.14), kind=kOutput, calls=%fused_computation.4 | convolution fusion | flops 2148532224 | bytes 6291456 | tf_op jit(solution)/shard_map/cond/branch_1_fun/dot_general | solution.py:84
  300.7 3.8 collective-permute-done.1
  304.5 3.2 fusion.4
  307.7 2.4 broadcast.206
  311.2 6.2 %all-to-all-start.1 = ((bf16[16,256,512]{2,1,0:T(8,128)(2,1)}), bf16[16,256,512]{2,1,0:T(8,128)(2,1)}, u32[]{:S(2)}, u32[]{:S(2)}) async-start(bf16[16,256,512]{2,1,0:T(8,128)(2,1)} %constant_dynamic-update-slice_fusion), calls=%async_computation.2 | async-start | bytes 8388608 | tf_op jit(solution)/shard_map/all_to_all | solution.py:106
  318.5 4.6 %conditional.2 = (f32[1024,1024]{1,0:T(8,128)}) conditional(s32[]{:T(128)} %convert_element_type.17, bf16[1024,1024]{1,0:T(8,128)(2,1)S(1)} %copy-done.4, bf16[1024,1024]{1,0:T(8,128)(2,1)S(1)} %copy-done.4), branch_computations={%region_2.3_spmd, %region_3.4_spmd} | conditional | flops 2147483648 | bytes 6291464 | solution.py:71
  318.7 4.4 %fusion.18 = f32[1024,1024]{1,0:T(8,128)} fusion(bf16[1024,1024]{1,0:T(8,128)(2,1)S(1)} %param.1), kind=kOutput, calls=%fused_computation.62 | convolution fusion | flops 2147483648 | bytes 6291456 | tf_op jit(solution)/shard_map/cond/branch_1_fun/dot_general | solution.py:73
  323.1 7.0 %fusion = f32[1,1,1024,1024]{3,2,1,0:T(8,128)} fusion(f32[1024,1024]{1,0:T(8,128)} %get-tuple-element.139, f32[1,1,1024,1024]{3,2,1,0:T(8,128)} %param.12), kind=kLoop, calls=%fused_computation.12 | loop fusion | flops 3145728 | bytes 12582912 | tf_op jit(solution)/shard_map/broadcast_in_dim | solution.py:110
  330.0 44.2 %all-to-all-done.1 = bf16[16,256,512]{2,1,0:T(8,128)(2,1)} async-done(((bf16[16,256,512]{2,1,0:T(8,128)(2,1)}), bf16[16,256,512]{2,1,0:T(8,128)(2,1)}, u32[]{:S(2)}, u32[]{:S(2)}) %all-to-all-start.1) | async-done | bytes 4194336 | tf_op jit(solution)/shard_map/all_to_all | solution.py:106
  374.3 2.8 gather_fusion.3
  (171 shorter events, 87.0 us)
Async XLA Ops:
  7.2 12.2 %copy-start = (s32[16,16]{1,0:T(8,128)S(1)}, s32[16,16]{1,0:T(8,128)}, u32[]{:S(2)}) copy-start(s32[16,16]{1,0:T(8,128)} %param.11) | copy-start | bytes 3076
  7.2 13.8 %copy-start.2 = (bf16[256,2048]{1,0:T(8,128)(2,1)S(1)}, bf16[256,2048]{1,0:T(8,128)(2,1)}, u32[]{:S(2)}) copy-start(bf16[256,2048]{1,0:T(8,128)(2,1)} %param.10) | copy-start | bytes 3145732
  9.7 58.6 %all-to-all-start = ((bf16[16,256,256]{2,1,0:T(8,128)(2,1)}), bf16[16,256,256]{2,1,0:T(8,128)(2,1)S(1)}, u32[]{:S(2)}, u32[]{:S(2)}) async-start(bf16[16,256,256]{2,1,0:T(8,128)(2,1)} %stack.2), calls=%async_computation | async-start | bytes 4194304 | tf_op jit(solution)/shard_map/all_to_all | solution.py:36
  19.3 268.7 %reduce-scatter.2.cloned.1.call-start = ((), (), s32[]{:S(2)}) async-start(), calls=%async_computation.3 | async-start | bytes 17825792 | tf_op jit(solution)/shard_map/reduce_scatter | solution.py:56
  135.2 159.6 %copy-start.3 = (bf16[1,1,1024,1024]{3,2,1,0:T(8,128)(2,1)S(1)}, bf16[1,1,1024,1024]{3,2,1,0:T(8,128)(2,1)}, u32[]{:S(2)}) copy-start(bf16[1,1,1024,1024]{3,2,1,0:T(8,128)(2,1)} %param.13) | copy-start | bytes 6291460
  288.0 2.9 collective-permute-start
  300.0 4.5 %collective-permute-start.1 = (bf16[1024,1024]{1,0:T(8,128)(2,1)}, bf16[1024,1024]{1,0:T(8,128)(2,1)}, u32[]{:S(2)}, u32[]{:S(2)}) collective-permute-start(bf16[1024,1024]{1,0:T(8,128)(2,1)} %get-tuple-element.140), channel_id=1, source_target_pairs={{0,16},{16,0},{32,48},{48,32},{64,80},{80,64},{96,112},{112,96},{1... | collective-permute-start | bytes 6291464 | tf_op jit(solution)/shard_map/ppermute | solution.py:12
  311.2 7.3 %copy-start.4 = (bf16[1024,1024]{1,0:T(8,128)(2,1)S(1)}, bf16[1024,1024]{1,0:T(8,128)(2,1)}, u32[]{:S(2)}) copy-start(bf16[1024,1024]{1,0:T(8,128)(2,1)} %maximum_select_fusion) | copy-start | bytes 6291460
  311.2 63.1 %all-to-all-start.1 = ((bf16[16,256,512]{2,1,0:T(8,128)(2,1)}), bf16[16,256,512]{2,1,0:T(8,128)(2,1)}, u32[]{:S(2)}, u32[]{:S(2)}) async-start(bf16[16,256,512]{2,1,0:T(8,128)(2,1)} %constant_dynamic-update-slice_fusion), calls=%async_computation.2 | async-start | bytes 8388608 | tf_op jit(solution)/shard_map/all_to_all | solution.py:106
  323.1 55.2 %copy-start.1 = (s32[16,16]{1,0:T(8,128)S(1)}, s32[16,16]{1,0:T(8,128)}, u32[]{:S(2)}) copy-start(s32[16,16]{1,0:T(8,128)} %param.11) | copy-start | bytes 3076
Sparse Core Ops, SparseCore 0:
  135.3 152.6 reduce-scatter.1
